TPU v7x, 32 devices: a whole 2x2x4 slice. The times are simulated.
32 devices in a mesh: group: 2 (over x), tile: 8 (over z, y), draw: 2 (over core).
Axes of the slice: x: 2, y: 2, z: 4, core: 2. Of those that a mesh axis runs over, the one named last changes fastest.
Arguments:
- inputs: bfloat16 [4, 32, 270, 256], P(('group', 'draw'), 'tile'), parts along dimension 0, may hold values from -6 to 6
- land_mask: int32 [32, 270], P('tile'), may hold values 0 or 1
- kernel: float32 [7, 7, 256], replicated, may hold values from -0.875 to 0.875
- conv_bias: float32 [256], replicated, may hold values from -3 to 3
- norm_gain: float32 [256], replicated, may hold values from 0.1 to 1.9
- norm_bias: float32 [256], replicated, may hold values from -3 to 3
- w_in: bfloat16 [256, 1024], replicated, may hold values from -0.375 to 0.375
- b_in: float32 [1024], replicated, may hold values from -3 to 3
- w_out: bfloat16 [1024, 256], replicated, may hold values from -0.1875 to 0.1875
- b_out: float32 [256], replicated, may hold values from -3 to 3
- layer_scale: float32 [256], replicated, may hold values from 0.1 to 1.9
- cotangent: bfloat16 [4, 32, 270, 256], P(('group', 'draw'), 'tile'), parts along dimension 0, may hold values from -6 to 6
Outputs:
- output: bfloat16 [4, 32, 270, 256], P(('group', 'draw'), 'tile'), parts along dimension 0
- input_grad: bfloat16 [4, 32, 270, 256], P(('group', 'draw'), 'tile'), parts along dimension 0
- kernel_grad: float32 [14, 7, 256], P('group'), parts along dimension 0
- w_in_grad: float32 [512, 1024], P('group'), parts along dimension 0
- w_out_grad: float32 [2048, 256], P('group'), parts along dimension 0
- b_in_grad: float32 [2048], P('group'), parts along dimension 0
- channel_grads: float32 [10, 256], P('group'), parts along dimension 0
There are 2 independent parts, one for each index of `group`. A program takes and returns all parts, laid end to end along the dimension named above; an argument that names none is the same for every part. Nothing has to cross between parts.
All inputs are finite; a program needn't handle non-finite values. No bound on the sum of `land_mask` on one device may be relied on, other than what follows from the above.
Results may differ from a plain program's by a relative error of at most 0.007.
Values may be sent and summed in bfloat16 or wider, within the bound.
A program may use at most 64 MiB of HBM per device.

v0:
```python
import jax
import jax.numpy as jnp
from jax import lax
from jax.sharding import PartitionSpec as P

ROOT_TERM = 0.7978845608028654
CUBIC = 0.044715
EPSILON = 1e-06


def with_halo(cells, sides, width):
    for axis, dim in sides:
        count = lax.axis_size(axis)
        ends = count - 1
        head = lax.slice_in_dim(cells, 0, width, axis=dim)
        tail = lax.slice_in_dim(cells, cells.shape[dim] - width, cells.shape[dim], axis=dim)
        cells = jnp.concatenate(
            [
                lax.ppermute(tail, axis, [(i, (i + 1) % count) for i in range(ends)]),
                cells,
                lax.ppermute(head, axis, [((i + 1) % count, i) for i in range(ends)]),
            ],
            axis=dim,
        )
    return cells


def lon_wrap(values):
    return jnp.concatenate([values[:, :, -3:], values, values[:, :, :3]], axis=2)


def apply_taps(padded, weights, height, breadth):
    total = jnp.zeros((padded.shape[0], height, breadth, padded.shape[3]), jnp.float32)
    for row_off in range(7):
        for col_off in range(7):
            total = (
                total
                + padded[:, row_off : row_off + height, col_off : col_off + breadth, :]
                * weights[row_off, col_off]
            )
    return total


def kernel_terms(padded, grad_map, height, breadth):
    rows_list = []
    for row_off in range(7):
        cells_list = []
        for col_off in range(7):
            window = padded[:, row_off : row_off + height, col_off : col_off + breadth, :]
            cells_list.append(jnp.sum(window * grad_map, axis=(0, 1, 2)))
        rows_list.append(jnp.stack(cells_list))
    return jnp.stack(rows_list)


def gelu_slope(hidden):
    inner = ROOT_TERM * (hidden + CUBIC * hidden * hidden * hidden)
    tanh_value = jnp.tanh(inner)
    return 0.5 * (1.0 + tanh_value) + 0.5 * hidden * (1.0 - tanh_value * tanh_value) * ROOT_TERM * (
        1.0 + 3.0 * CUBIC * hidden * hidden
    )


def grad_extend(values):
    return with_halo(values, (("tile", 1),), 3)


def per_device(
    inputs,
    land_mask,
    kernel,
    conv_bias,
    norm_gain,
    norm_bias,
    w_in,
    b_in,
    w_out,
    b_out,
    layer_scale,
    cotangent,
):
    height = inputs.shape[1]
    breadth = inputs.shape[2]
    channels = inputs.shape[3]
    padded_state = with_halo(inputs, (("tile", 1),), 3)
    wrapped = lon_wrap(padded_state.astype(jnp.float32))
    conv_out = apply_taps(wrapped, kernel, height, breadth) + conv_bias
    center = jnp.mean(conv_out, axis=-1, keepdims=True)
    deviation = conv_out - center
    inv_std = lax.rsqrt(jnp.mean(deviation * deviation, axis=-1, keepdims=True) + EPSILON)
    unit = deviation * inv_std
    normed = (unit * norm_gain + norm_bias).astype(jnp.bfloat16).reshape(-1, channels)
    hidden = jnp.dot(normed, w_in, preferred_element_type=jnp.float32) + b_in
    inner = ROOT_TERM * (hidden + CUBIC * hidden * hidden * hidden)
    activated = (0.5 * hidden * (1.0 + jnp.tanh(inner))).astype(jnp.bfloat16)
    mixed = (jnp.dot(activated, w_out, preferred_element_type=jnp.float32) + b_out).reshape(
        inputs.shape
    )
    ocean = land_mask.astype(jnp.float32)[None, :, :, None]
    output = (inputs.astype(jnp.float32) + ocean * layer_scale * mixed).astype(jnp.bfloat16)
    upstream = cotangent.astype(jnp.float32)
    scale_part = jnp.sum(ocean * upstream * mixed, axis=(0, 1, 2))
    grad_mixed = (ocean * layer_scale * upstream).astype(jnp.bfloat16).reshape(-1, channels)
    out_bias_part = jnp.sum(grad_mixed.astype(jnp.float32), axis=0)
    w_out_part = lax.dot_general(
        activated, grad_mixed, (((0,), (0,)), ((), ())), preferred_element_type=jnp.float32
    )
    grad_act = lax.dot_general(
        grad_mixed, w_out, (((1,), (1,)), ((), ())), preferred_element_type=jnp.float32
    )
    grad_hidden = (grad_act * gelu_slope(hidden)).astype(jnp.bfloat16)
    w_in_part = lax.dot_general(
        normed, grad_hidden, (((0,), (0,)), ((), ())), preferred_element_type=jnp.float32
    )
    hidden_bias_part = jnp.sum(grad_hidden.astype(jnp.float32), axis=0)
    grad_normed = lax.dot_general(
        grad_hidden, w_in, (((1,), (1,)), ((), ())), preferred_element_type=jnp.float32
    ).reshape(inputs.shape)
    gain_part = jnp.sum(grad_normed * unit, axis=(0, 1, 2))
    nbias_part = jnp.sum(grad_normed, axis=(0, 1, 2))
    scaled = grad_normed * norm_gain
    grad_conv = (
        inv_std
        * (
            scaled
            - jnp.mean(scaled, axis=-1, keepdims=True)
            - unit * jnp.mean(scaled * unit, axis=-1, keepdims=True)
        )
    ).astype(jnp.bfloat16)
    grad_float = grad_conv.astype(jnp.float32)
    conv_bias_part = jnp.sum(grad_float, axis=(0, 1, 2))
    kernel_part = kernel_terms(wrapped, grad_float, height, breadth)
    grad_padded = lon_wrap(grad_extend(grad_conv).astype(jnp.float32))
    input_grad = (upstream + apply_taps(grad_padded, kernel[::-1, ::-1], height, breadth)).astype(
        jnp.bfloat16
    )
    channel_part = jnp.stack([conv_bias_part, gain_part, nbias_part, out_bias_part, scale_part])
    kernel_sum, w_in_sum, w_out_sum, hidden_sum, channel_sum = lax.psum(
        (kernel_part, w_in_part, w_out_part, hidden_bias_part, channel_part), ("tile", "draw")
    )
    total_cells = inputs.shape[0] * lax.axis_size("draw") * height * lax.axis_size("tile") * breadth
    factor = 1.0 / jnp.sqrt(jnp.float32(total_cells))
    return (
        output,
        input_grad,
        kernel_sum * factor,
        w_in_sum * factor,
        w_out_sum * factor,
        hidden_sum * factor,
        channel_sum * factor,
    )


def solution(mesh):
    placed = (
        P(("group", "draw"), "tile", None, None),
        P("tile", None),
        P(),
        P(),
        P(),
        P(),
        P(),
        P(),
        P(),
        P(),
        P(),
        P(("group", "draw"), "tile", None, None),
    )
    return jax.shard_map(
        per_device,
        mesh=mesh,
        in_specs=placed,
        out_specs=(
            P(("group", "draw"), "tile", None, None),
            P(("group", "draw"), "tile", None, None),
            P("group", None, None),
            P("group", None),
            P("group", None),
            P("group"),
            P("group", None),
        ),
        check_vma=False,
    )
```

profile of v0, /device:TPU:0, one launch (start us, length us, event | category | flops | bytes accessed | tf_op | source)
XLA Modules:
  0.0 275.7 jit_solution(4740820683694021550)
XLA Ops:
  7.2 0.0 copy-start
  7.2 0.0 all-reduce.4.cloned.1.call-start
  7.2 1.2 copy.24
  8.4 0.0 copy-start.9
  8.4 0.0 copy-start.51
  8.4 0.1 fusion.237
  8.5 4.9 %collective-permute-start = (bf16[1,3,270,256]{3,2,1,0:T(8,128)(2,1)S(1)}, bf16[1,3,270,256]{3,2,1,0:T(8,128)(2,1)S(1)}, u32[]{:S(2)}, u32[]{:S(2)}) collective-permute-start(bf16[1,3,270,256]{3,2,1,0:T(8,128)(2,1)S(1)} %get-tuple-element.91), channel_id=1, source_target_pairs={{0,2},{2,4},{4,6},{6,8},{8,10},{10,12},{12,14},{1,3},{3,5},{5,7},{... | collective-permute-start | bytes 1244168 | tf_op jit(solution)/shard_map/ppermute | solution.py:19
  13.4 1.3 collective-permute-start.1
  15.0 0.0 copy-start.91
  15.0 16.2 %collective-permute-done = bf16[1,3,270,256]{3,2,1,0:T(8,128)(2,1)S(1)} collective-permute-done((bf16[1,3,270,256]{3,2,1,0:T(8,128)(2,1)S(1)}, bf16[1,3,270,256]{3,2,1,0:T(8,128)(2,1)S(1)}, u32[]{:S(2)}, u32[]{:S(2)}) %collective-permute-start) | collective-permute-done | bytes 414752 | tf_op jit(solution)/shard_map/ppermute | solution.py:19
  31.2 0.2 maximum_convert_fusion
  31.7 9.9 %fusion.233 = (f32[4,270]{1,0:T(4,128)S(1)}, f32[1,4,270,256]{3,2,1,0:T(8,128)S(1)}) fusion(f32[256]{0:T(256)S(1)} %copy-done.91, f32[256]{0:T(256)S(1)} %bitcast.185, f32[1,10,3,256]{3,2,1,0:T(4,128)S(1)} %get-tuple-element.84, f32[1,10,270,256]{3,2,1,0:T(8,128)S(1)} %maximum_convert_fusion, f32[256]{0:T(256)S(1)} %bitcast.187, f32[256]{0:T(256)S(1)} %bitcast.131, ...), kind=kLoop, calls=%fused_computation.447 | loop fusion | flops 38982600 | bytes 11827424 | tf_op jit(solution)/shard_map/reduce_sum | solution.py:87
  41.5 0.0 copy-start.10
  41.6 0.0 copy-start.92
  41.6 0.5 multiply_reduce_fusion.2
  42.1 0.5 copy-done.3
  42.5 1.2 add_convert_fusion
  43.7 2.0 reshape.497
  45.7 4.8 %multiply_convert_fusion = (bf16[1080,1024]{1,0:T(8,128)(2,1)S(1)}, f32[1080,1024]{1,0:T(8,128)}) fusion(f32[1024]{0:T(1024)S(1)} %copy-done.96, bf16[1080,256]{1,0:T(8,128)(2,1)} %reshape.497, bf16[256,1024]{1,0:T(8,128)(2,1)S(1)} %copy-done), kind=kOutput, calls=%fused_computation.140 | convolution fusion | flops 577290240 | bytes 7716864 | tf_op jit(solution)/shard_map/dot_general | solution.py:92
  50.6 1.4 copy-done.99
  52.0 1.9 convolution_add_fusion.1
  53.8 2.5 reshape.498
  56.3 3.6 %fusion.11 = (f32[256]{0:T(256)}, bf16[1,4,270,256]{3,2,1,0:T(8,128)(2,1)}, f32[256]{0:T(256)}, bf16[1,4,270,256]{3,2,1,0:T(8,128)(2,1)}) fusion(f32[1,4,270,256]{3,2,1,0:T(8,128)} %reshape.498, f32[4,270]{1,0:T(4,128)S(1)} %convert_element_type.63, bf16[1,4,270,256]{3,1,2,0:T(4,128)(2,1)} %param.23, f32[256]{0:T(256)S(1)} %copy-done.93, ...), kind=kLoop, calls=%fused_computation.154 | loop fusion | flops 3593728 | bytes 3325152 | tf_op jit(solution)/shard_map/reduce_sum | solution.py:101
  60.0 2.0 reshape.499
  62.0 3.7 %fusion.242 = f32[1024,256]{1,0:T(8,128)} fusion(bf16[1080,1024]{1,0:T(8,128)(2,1)} %copy-done.99, bf16[1080,256]{1,0:T(8,128)(2,1)} %reshape.499), kind=kOutput, calls=%fused_computation.456 | convolution fusion | flops 566231040 | bytes 3813376 | tf_op jit(solution)/shard_map/dot_general | solution.py:104
  65.7 0.0 copy-start.7
  65.8 3.8 %convert_reduce_fusion.1 = (f32[1024]{0:T(1024)}, bf16[1080,1024]{1,0:T(8,128)(2,1)S(1)}) fusion(f32[1080,1024]{1,0:T(8,128)S(1)} %copy-done.100, bf16[1080,256]{1,0:T(8,128)(2,1)S(1)} %copy-done.8, bf16[1024,256]{1,0:T(8,128)(2,1)S(1)} %copy-done.95), kind=kOutput, calls=%fused_computation.139 | convolution fusion | flops 589454336 | bytes 7716864 | tf_op jit(solution)/shard_map/dot_general | solution.py:107
  69.6 1.4 copy-done.98
  71.0 1.9 fusion.241
  72.9 4.0 %fusion.231 = (f32[256]{0:T(256)}, f32[1080]{0:T(1024)S(1)}, f32[1080,256]{1,0:T(8,128)}) fusion(f32[256]{0:T(256)S(1)} %copy-done.10, bf16[1080,1024]{1,0:T(8,128)(2,1)} %copy-done.98, bf16[256,1024]{1,0:T(8,128)(2,1)S(1)} %copy-done), kind=kOutput, calls=%fused_computation.446 | convolution fusion | flops 567059136 | bytes 3848416 | tf_op jit(solution)/shard_map/dot_general | solution.py:115
  76.9 2.4 reshape.500
  79.2 2.7 multiply_reduce_fusion
  82.0 0.1 div.17
  82.1 2.0 fusion.57
  84.1 2.1 fusion.55
  86.2 2.4 fusion.59
  88.6 2.3 fusion.60
  90.9 2.0 fusion.56
  92.9 2.5 fusion.58
  95.8 0.0 copy-start.52
  95.8 0.0 copy-start.53
  95.8 0.0 copy-start.54
  95.8 0.1 fusion.236
  95.9 0.2 copy-done.77
  96.1 0.0 copy-done.80
  96.1 0.7 stack.217
  96.9 0.7 stack.226
  97.6 0.7 stack.235
  98.7 0.7 stack.279
  99.4 62.4 %all-reduce = (f32[7,7,256]{2,1,0:T(8,128)S(1)}, f32[1024]{0:T(1024)S(1)}, f32[5,256]{1,0:T(8,128)S(1)}) all-reduce(f32[7,7,256]{2,1,0:T(8,128)S(1)} %constant_dynamic-update-slice_fusion, f32[1024]{0:T(1024)S(1)} %copy-done.82, f32[5,256]{1,0:T(8,128)S(1)} %stack.279), channel_id=1, replica_groups=mesh['group'=2,'tile'=8,'draw'=2] {'tile','draw'}, use_global_device_ids=true, to_apply=%region_53.0 | all-reduce | flops 14848 | bytes 118784 | tf_op jit(solution)/shard_map/psum | solution.py:137
  161.8 0.6 broadcast_multiply_fusion.3
  162.4 1.3 collective-permute-start.2
  163.7 1.3 collective-permute-start.3
  165.1 1.1 copy.29
  166.1 0.0 all-reduce.4.cloned.1.call-update
  166.2 0.6 broadcast_multiply_fusion.7
  166.8 0.6 broadcast_multiply_fusion.2
  167.6 13.8 %collective-permute-done.2 = bf16[1,3,270,256]{3,2,1,0:T(8,128)(2,1)S(1)} collective-permute-done((bf16[1,3,270,256]{3,2,1,0:T(8,128)(2,1)S(1)}, bf16[1,3,270,256]{3,2,1,0:T(8,128)(2,1)S(1)}, u32[]{:S(2)}, u32[]{:S(2)}) %collective-permute-start.2) | collective-permute-done | bytes 414752 | tf_op jit(solution)/shard_map/ppermute | solution.py:19
  181.4 0.2 maximum_convert_fusion.1
  181.9 9.5 %fusion.9 = bf16[1,4,270,256]{3,2,1,0:T(8,128)(2,1)S(1)} fusion(f32[1,10,3,256]{3,2,1,0:T(4,128)S(1)} %get-tuple-element.82, f32[1,10,270,256]{3,2,1,0:T(8,128)S(1)} %maximum_convert_fusion.1, f32[1,10,3,256]{3,2,1,0:T(4,128)S(1)} %get-tuple-element.81, f32[256]{0:T(256)S(1)} %bitcast.186, f32[256]{0:T(256)S(1)} %bitcast.188, f32[256]{0:T(256)S(1)} %bitcast.132, ...), kind=kLoop, calls=%fused_computation.152 | loop fusion | flops 39260160 | bytes 11822080 | tf_op jit(solution)/shard_map/convert_element_type | solution.py:133
  191.4 1.1 copy.30
  192.5 72.9 %all-reduce.4.cloned.1.call-done = (f32[256,1024]{1,0:T(8,128)}, f32[1024,256]{1,0:T(8,128)}) async-done(((f32[256,1024]{1,0:T(8,128)}, f32[1024,256]{1,0:T(8,128)}), (f32[256,1024]{1,0:T(8,128)}, f32[1024,256]{1,0:T(8,128)})) %all-reduce.4.cloned.1.call-update) | async-done | bytes 2097168 | tf_op jit(solution)/shard_map/psum | solution.py:137
  265.4 2.4 broadcast_multiply_fusion
  267.8 1.1 broadcast_multiply_fusion.1
  (210 shorter events, 0.6 us)
Async XLA Ops:
  7.2 38.5 %copy-start = (bf16[256,1024]{1,0:T(8,128)(2,1)S(1)}, bf16[256,1024]{1,0:T(8,128)(2,1)}, u32[]{:S(2)}) copy-start(bf16[256,1024]{1,0:T(8,128)(2,1)} %param.18) | copy-start | bytes 1572868
  7.2 258.2 %all-reduce.4.cloned.1.call-start = ((), (), s32[]{:S(2)}) async-start(), calls=%async_computation | async-start | bytes 4194304 | tf_op jit(solution)/shard_map/psum | solution.py:137
  8.4 6.3 %copy-start.9 = (f32[7,7,256]{2,1,0:T(8,128)S(1)}, f32[7,7,256]{2,1,0:T(8,128)}, u32[]{:S(2)}) copy-start(f32[7,7,256]{2,1,0:T(8,128)} %param.14) | copy-start | bytes 150532
  8.4 6.3 %copy-start.51 = (s32[4,270]{1,0:T(4,128)S(1)}, s32[4,270]{1,0:T(4,128)}, u32[]{:S(2)}) copy-start(s32[4,270]{1,0:T(4,128)} %param.13) | copy-start | bytes 12964
  8.5 22.7 %collective-permute-start = (bf16[1,3,270,256]{3,2,1,0:T(8,128)(2,1)S(1)}, bf16[1,3,270,256]{3,2,1,0:T(8,128)(2,1)S(1)}, u32[]{:S(2)}, u32[]{:S(2)}) collective-permute-start(bf16[1,3,270,256]{3,2,1,0:T(8,128)(2,1)S(1)} %get-tuple-element.91), channel_id=1, source_target_pairs={{0,2},{2,4},{4,6},{6,8},{8,10},{10,12},{12,14},{1,3},{3,5},{5,7},{... | collective-permute-start | bytes 1244168 | tf_op jit(solution)/shard_map/ppermute | solution.py:19
  13.4 17.8 %collective-permute-start.1 = (bf16[1,3,270,256]{3,2,1,0:T(8,128)(2,1)S(1)}, bf16[1,3,270,256]{3,2,1,0:T(8,128)(2,1)S(1)}, u32[]{:S(2)}, u32[]{:S(2)}) collective-permute-start(bf16[1,3,270,256]{3,2,1,0:T(8,128)(2,1)S(1)} %get-tuple-element.92), channel_id=1, source_target_pairs={{2,0},{4,2},{6,4},{8,6},{10,8},{12,10},{14,12},{3,1},{5,3},{7,5},{... | collective-permute-start | bytes 1244168 | tf_op jit(solution)/shard_map/ppermute | solution.py:21
  14.8 16.7 %copy-start.11 = (f32[1,1,256]{2,1,0:T(1,128)}, f32[1,1,256]{2,1,0:T(1,128)S(1)}, u32[]{:S(2)}) copy-start(f32[1,1,256]{2,1,0:T(1,128)S(1)} %get-tuple-element.141) | copy-start | bytes 3076
  14.8 16.7 %copy-start.13 = (f32[1,1,256]{2,1,0:T(1,128)}, f32[1,1,256]{2,1,0:T(1,128)S(1)}, u32[]{:S(2)}) copy-start(f32[1,1,256]{2,1,0:T(1,128)S(1)} %get-tuple-element.112) | copy-start | bytes 3076
  14.8 16.7 %copy-start.15 = (f32[1,1,256]{2,1,0:T(1,128)}, f32[1,1,256]{2,1,0:T(1,128)S(1)}, u32[]{:S(2)}) copy-start(f32[1,1,256]{2,1,0:T(1,128)S(1)} %get-tuple-element.113) | copy-start | bytes 3076
  14.8 16.7 %copy-start.17 = (f32[1,1,256]{2,1,0:T(1,128)}, f32[1,1,256]{2,1,0:T(1,128)S(1)}, u32[]{:S(2)}) copy-start(f32[1,1,256]{2,1,0:T(1,128)S(1)} %get-tuple-element.114) | copy-start | bytes 3076
  14.8 16.7 %copy-start.19 = (f32[1,1,256]{2,1,0:T(1,128)}, f32[1,1,256]{2,1,0:T(1,128)S(1)}, u32[]{:S(2)}) copy-start(f32[1,1,256]{2,1,0:T(1,128)S(1)} %get-tuple-element.115) | copy-start | bytes 3076
  14.9 16.7 %copy-start.21 = (f32[1,1,256]{2,1,0:T(1,128)}, f32[1,1,256]{2,1,0:T(1,128)S(1)}, u32[]{:S(2)}) copy-start(f32[1,1,256]{2,1,0:T(1,128)S(1)} %get-tuple-element.116) | copy-start | bytes 3076
  14.9 16.7 %copy-start.23 = (f32[1,1,256]{2,1,0:T(1,128)}, f32[1,1,256]{2,1,0:T(1,128)S(1)}, u32[]{:S(2)}) copy-start(f32[1,1,256]{2,1,0:T(1,128)S(1)} %get-tuple-element.117) | copy-start | bytes 3076
  14.9 16.7 %copy-start.25 = (f32[1,1,256]{2,1,0:T(1,128)}, f32[1,1,256]{2,1,0:T(1,128)S(1)}, u32[]{:S(2)}) copy-start(f32[1,1,256]{2,1,0:T(1,128)S(1)} %get-tuple-element.118) | copy-start | bytes 3076
  14.9 16.7 %copy-start.27 = (f32[1,1,256]{2,1,0:T(1,128)}, f32[1,1,256]{2,1,0:T(1,128)S(1)}, u32[]{:S(2)}) copy-start(f32[1,1,256]{2,1,0:T(1,128)S(1)} %get-tuple-element.119) | copy-start | bytes 3076
  14.9 16.7 %copy-start.29 = (f32[1,1,256]{2,1,0:T(1,128)}, f32[1,1,256]{2,1,0:T(1,128)S(1)}, u32[]{:S(2)}) copy-start(f32[1,1,256]{2,1,0:T(1,128)S(1)} %get-tuple-element.120) | copy-start | bytes 3076
  14.9 16.7 %copy-start.31 = (f32[1,1,256]{2,1,0:T(1,128)}, f32[1,1,256]{2,1,0:T(1,128)S(1)}, u32[]{:S(2)}) copy-start(f32[1,1,256]{2,1,0:T(1,128)S(1)} %get-tuple-element.121) | copy-start | bytes 3076
  14.9 16.7 %copy-start.33 = (f32[1,1,256]{2,1,0:T(1,128)}, f32[1,1,256]{2,1,0:T(1,128)S(1)}, u32[]{:S(2)}) copy-start(f32[1,1,256]{2,1,0:T(1,128)S(1)} %get-tuple-element.122) | copy-start | bytes 3076
  14.9 16.7 %copy-start.35 = (f32[1,1,256]{2,1,0:T(1,128)}, f32[1,1,256]{2,1,0:T(1,128)S(1)}, u32[]{:S(2)}) copy-start(f32[1,1,256]{2,1,0:T(1,128)S(1)} %get-tuple-element.123) | copy-start | bytes 3076
  14.9 16.7 %copy-start.37 = (f32[1,1,256]{2,1,0:T(1,128)}, f32[1,1,256]{2,1,0:T(1,128)S(1)}, u32[]{:S(2)}) copy-start(f32[1,1,256]{2,1,0:T(1,128)S(1)} %get-tuple-element.124) | copy-start | bytes 3076
  14.9 16.7 %copy-start.39 = (f32[1,1,256]{2,1,0:T(1,128)}, f32[1,1,256]{2,1,0:T(1,128)S(1)}, u32[]{:S(2)}) copy-start(f32[1,1,256]{2,1,0:T(1,128)S(1)} %get-tuple-element.125) | copy-start | bytes 3076
  15.0 16.7 %copy-start.41 = (f32[1,1,256]{2,1,0:T(1,128)}, f32[1,1,256]{2,1,0:T(1,128)S(1)}, u32[]{:S(2)}) copy-start(f32[1,1,256]{2,1,0:T(1,128)S(1)} %get-tuple-element.126) | copy-start | bytes 3076
  15.0 16.7 %copy-start.43 = (f32[1,1,256]{2,1,0:T(1,128)}, f32[1,1,256]{2,1,0:T(1,128)S(1)}, u32[]{:S(2)}) copy-start(f32[1,1,256]{2,1,0:T(1,128)S(1)} %get-tuple-element.127) | copy-start | bytes 3076
  15.0 16.7 %copy-start.45 = (f32[1,1,256]{2,1,0:T(1,128)}, f32[1,1,256]{2,1,0:T(1,128)S(1)}, u32[]{:S(2)}) copy-start(f32[1,1,256]{2,1,0:T(1,128)S(1)} %get-tuple-element.128) | copy-start | bytes 3076
  15.0 16.7 %copy-start.47 = (f32[1,1,256]{2,1,0:T(1,128)}, f32[1,1,256]{2,1,0:T(1,128)S(1)}, u32[]{:S(2)}) copy-start(f32[1,1,256]{2,1,0:T(1,128)S(1)} %get-tuple-element.129) | copy-start | bytes 3076
  15.0 16.7 %copy-start.49 = (f32[1,1,256]{2,1,0:T(1,128)}, f32[1,1,256]{2,1,0:T(1,128)S(1)}, u32[]{:S(2)}) copy-start(f32[1,1,256]{2,1,0:T(1,128)S(1)} %get-tuple-element.130) | copy-start | bytes 3076
  15.0 16.7 %copy-start.91 = (f32[256]{0:T(256)S(1)}, f32[256]{0:T(256)}, u32[]{:S(2)}) copy-start(f32[256]{0:T(256)} %param.15) | copy-start | bytes 3076
  42.5 3.2 %copy-start.96 = (f32[1024]{0:T(1024)S(1)}, f32[1024]{0:T(1024)}, u32[]{:S(2)}) copy-start(f32[1024]{0:T(1024)} %param.19) | copy-start | bytes 12292
  45.7 6.2 %copy-start.94 = (bf16[1024,256]{1,0:T(8,128)(2,1)S(1)}, bf16[1024,256]{1,0:T(8,128)(2,1)}, u32[]{:S(2)}) copy-start(bf16[1024,256]{1,0:T(8,128)(2,1)} %param.20) | copy-start | bytes 1572868
  45.7 6.2 %copy-start.97 = (f32[256]{0:T(256)S(1)}, f32[256]{0:T(256)}, u32[]{:S(2)}) copy-start(f32[256]{0:T(256)} %param.21) | copy-start | bytes 3076
  62.0 3.8 %copy-start.8 = (bf16[1080,256]{1,0:T(8,128)(2,1)S(1)}, bf16[1080,256]{1,0:T(8,128)(2,1)}, u32[]{:S(2)}) copy-start(bf16[1080,256]{1,0:T(8,128)(2,1)} %reshape.499) | copy-start | bytes 1658884
  62.0 3.8 %copy-start.95 = (bf16[1024,256]{1,0:T(8,128)(2,1)S(1)}, bf16[1024,256]{1,0:T(8,128)(2,1)}, u32[]{:S(2)}) copy-start(bf16[1024,256]{1,0:T(8,128)(2,1)} %param.20) | copy-start | bytes 1572868
  62.0 3.8 %copy-start.100 = (f32[1080,1024]{1,0:T(8,128)S(1)}, f32[1080,1024]{1,0:T(8,128)}, u32[]{:S(2)}) copy-start(f32[1080,1024]{1,0:T(8,128)} %get-tuple-element.143) | copy-start | bytes 13271044
  65.7 5.2 %copy-start.7 = (bf16[1080,256]{1,0:T(8,128)(2,1)S(1)}, bf16[1080,256]{1,0:T(8,128)(2,1)}, u32[]{:S(2)}) copy-start(bf16[1080,256]{1,0:T(8,128)(2,1)} %reshape.497) | copy-start | bytes 1658884
  84.1 11.3 %copy-start.1 = (bf16[1,4,270,256]{3,2,1,0:T(8,128)(2,1)}, bf16[1,4,270,256]{3,2,1,0:T(8,128)(2,1)S(1)}, u32[]{:S(2)}) copy-start(bf16[1,4,270,256]{3,2,1,0:T(8,128)(2,1)S(1)} %get-tuple-element.78) | copy-start | bytes 1658884
  95.8 2.9 %copy-start.52 = (f32[256]{0:T(256)S(1)}, f32[256]{0:T(256)}, u32[]{:S(2)}) copy-start(f32[256]{0:T(256)} %get-tuple-element.85) | copy-start | bytes 3076
  95.8 2.9 %copy-start.53 = (f32[256]{0:T(256)S(1)}, f32[256]{0:T(256)}, u32[]{:S(2)}) copy-start(f32[256]{0:T(256)} %get-tuple-element.87) | copy-start | bytes 3076
  95.8 2.9 %copy-start.54 = (f32[256]{0:T(256)S(1)}, f32[256]{0:T(256)}, u32[]{:S(2)}) copy-start(f32[256]{0:T(256)} %get-tuple-element.65) | copy-start | bytes 3076
  95.8 3.6 %copy-start.82 = (f32[1024]{0:T(1024)S(1)}, f32[1024]{0:T(1024)}, u32[]{:S(2)}) copy-start(f32[1024]{0:T(1024)} %get-tuple-element.145) | copy-start | bytes 12292
  95.8 69.2 %copy-start.4 = (bf16[1,4,270,256]{3,2,1,0:T(8,128)(2,1)S(1)}, bf16[1,4,270,256]{3,2,1,0:T(8,128)(2,1)}, u32[]{:S(2)}) copy-start(bf16[1,4,270,256]{3,2,1,0:T(8,128)(2,1)} %get-tuple-element.86) | copy-start | bytes 1658884
  162.4 19.0 %collective-permute-start.2 = (bf16[1,3,270,256]{3,2,1,0:T(8,128)(2,1)S(1)}, bf16[1,3,270,256]{3,2,1,0:T(8,128)(2,1)S(1)}, u32[]{:S(2)}, u32[]{:S(2)}) collective-permute-start(bf16[1,3,270,256]{3,2,1,0:T(8,128)(2,1)S(1)} %get-tuple-element.89), channel_id=1, source_target_pairs={{0,2},{2,4},{4,6},{6,8},{8,10},{10,12},{12,14},{1,3},{3,5},{5,7},{... | collective-permute-start | bytes 1244168 | tf_op jit(solution)/shard_map/ppermute | solution.py:19
  163.7 17.7 %collective-permute-start.3 = (bf16[1,3,270,256]{3,2,1,0:T(8,128)(2,1)S(1)}, bf16[1,3,270,256]{3,2,1,0:T(8,128)(2,1)S(1)}, u32[]{:S(2)}, u32[]{:S(2)}) collective-permute-start(bf16[1,3,270,256]{3,2,1,0:T(8,128)(2,1)S(1)} %get-tuple-element.90), channel_id=1, source_target_pairs={{2,0},{4,2},{6,4},{8,6},{10,8},{12,10},{14,12},{3,1},{5,3},{7,5},{... | collective-permute-start | bytes 1244168 | tf_op jit(solution)/shard_map/ppermute | solution.py:21
  166.1 15.3 %copy-start.2 = (bf16[1,4,270,256]{3,2,1,0:T(8,128)(2,1)S(1)}, bf16[1,4,270,256]{3,2,1,0:T(8,128)(2,1)}, u32[]{:S(2)}) copy-start(bf16[1,4,270,256]{3,2,1,0:T(8,128)(2,1)} %copy-done.1) | copy-start | bytes 1658884
  167.4 14.3 %copy-start.5 = (bf16[1,4,270,256]{3,1,2,0:T(4,128)(2,1)S(1)}, bf16[1,4,270,256]{3,1,2,0:T(4,128)(2,1)}, u32[]{:S(2)}) copy-start(bf16[1,4,270,256]{3,1,2,0:T(4,128)(2,1)} %param.23) | copy-start | bytes 1658884
  167.4 14.3 %copy-start.12 = (f32[1,1,256]{2,1,0:T(1,128)S(1)}, f32[1,1,256]{2,1,0:T(1,128)}, u32[]{:S(2)}) copy-start(f32[1,1,256]{2,1,0:T(1,128)} %copy-done.11) | copy-start | bytes 3076
  167.4 14.3 %copy-start.14 = (f32[1,1,256]{2,1,0:T(1,128)S(1)}, f32[1,1,256]{2,1,0:T(1,128)}, u32[]{:S(2)}) copy-start(f32[1,1,256]{2,1,0:T(1,128)} %copy-done.13) | copy-start | bytes 3076
  167.4 14.3 %copy-start.16 = (f32[1,1,256]{2,1,0:T(1,128)S(1)}, f32[1,1,256]{2,1,0:T(1,128)}, u32[]{:S(2)}) copy-start(f32[1,1,256]{2,1,0:T(1,128)} %copy-done.15) | copy-start | bytes 3076
  167.4 14.3 %copy-start.18 = (f32[1,1,256]{2,1,0:T(1,128)S(1)}, f32[1,1,256]{2,1,0:T(1,128)}, u32[]{:S(2)}) copy-start(f32[1,1,256]{2,1,0:T(1,128)} %copy-done.17) | copy-start | bytes 3076
  167.4 14.3 %copy-start.20 = (f32[1,1,256]{2,1,0:T(1,128)S(1)}, f32[1,1,256]{2,1,0:T(1,128)}, u32[]{:S(2)}) copy-start(f32[1,1,256]{2,1,0:T(1,128)} %copy-done.19) | copy-start | bytes 3076
  167.4 14.3 %copy-start.22 = (f32[1,1,256]{2,1,0:T(1,128)S(1)}, f32[1,1,256]{2,1,0:T(1,128)}, u32[]{:S(2)}) copy-start(f32[1,1,256]{2,1,0:T(1,128)} %copy-done.21) | copy-start | bytes 3076
  167.4 14.3 %copy-start.24 = (f32[1,1,256]{2,1,0:T(1,128)S(1)}, f32[1,1,256]{2,1,0:T(1,128)}, u32[]{:S(2)}) copy-start(f32[1,1,256]{2,1,0:T(1,128)} %copy-done.23) | copy-start | bytes 3076
  167.4 14.3 %copy-start.26 = (f32[1,1,256]{2,1,0:T(1,128)S(1)}, f32[1,1,256]{2,1,0:T(1,128)}, u32[]{:S(2)}) copy-start(f32[1,1,256]{2,1,0:T(1,128)} %copy-done.25) | copy-start | bytes 3076
  167.5 14.3 %copy-start.28 = (f32[1,1,256]{2,1,0:T(1,128)S(1)}, f32[1,1,256]{2,1,0:T(1,128)}, u32[]{:S(2)}) copy-start(f32[1,1,256]{2,1,0:T(1,128)} %copy-done.27) | copy-start | bytes 3076
  167.5 14.3 %copy-start.30 = (f32[1,1,256]{2,1,0:T(1,128)S(1)}, f32[1,1,256]{2,1,0:T(1,128)}, u32[]{:S(2)}) copy-start(f32[1,1,256]{2,1,0:T(1,128)} %copy-done.29) | copy-start | bytes 3076
  167.5 14.3 %copy-start.32 = (f32[1,1,256]{2,1,0:T(1,128)S(1)}, f32[1,1,256]{2,1,0:T(1,128)}, u32[]{:S(2)}) copy-start(f32[1,1,256]{2,1,0:T(1,128)} %copy-done.31) | copy-start | bytes 3076
  167.5 14.3 %copy-start.34 = (f32[1,1,256]{2,1,0:T(1,128)S(1)}, f32[1,1,256]{2,1,0:T(1,128)}, u32[]{:S(2)}) copy-start(f32[1,1,256]{2,1,0:T(1,128)} %copy-done.33) | copy-start | bytes 3076
  167.5 14.3 %copy-start.36 = (f32[1,1,256]{2,1,0:T(1,128)S(1)}, f32[1,1,256]{2,1,0:T(1,128)}, u32[]{:S(2)}) copy-start(f32[1,1,256]{2,1,0:T(1,128)} %copy-done.35) | copy-start | bytes 3076
  167.5 14.3 %copy-start.38 = (f32[1,1,256]{2,1,0:T(1,128)S(1)}, f32[1,1,256]{2,1,0:T(1,128)}, u32[]{:S(2)}) copy-start(f32[1,1,256]{2,1,0:T(1,128)} %copy-done.37) | copy-start | bytes 3076
  167.5 14.3 %copy-start.40 = (f32[1,1,256]{2,1,0:T(1,128)S(1)}, f32[1,1,256]{2,1,0:T(1,128)}, u32[]{:S(2)}) copy-start(f32[1,1,256]{2,1,0:T(1,128)} %copy-done.39) | copy-start | bytes 3076
  167.5 14.3 %copy-start.42 = (f32[1,1,256]{2,1,0:T(1,128)S(1)}, f32[1,1,256]{2,1,0:T(1,128)}, u32[]{:S(2)}) copy-start(f32[1,1,256]{2,1,0:T(1,128)} %copy-done.41) | copy-start | bytes 3076
  167.5 14.3 %copy-start.44 = (f32[1,1,256]{2,1,0:T(1,128)S(1)}, f32[1,1,256]{2,1,0:T(1,128)}, u32[]{:S(2)}) copy-start(f32[1,1,256]{2,1,0:T(1,128)} %copy-done.43) | copy-start | bytes 3076
  167.5 14.3 %copy-start.46 = (f32[1,1,256]{2,1,0:T(1,128)S(1)}, f32[1,1,256]{2,1,0:T(1,128)}, u32[]{:S(2)}) copy-start(f32[1,1,256]{2,1,0:T(1,128)} %copy-done.45) | copy-start | bytes 3076
  167.6 14.3 %copy-start.48 = (f32[1,1,256]{2,1,0:T(1,128)S(1)}, f32[1,1,256]{2,1,0:T(1,128)}, u32[]{:S(2)}) copy-start(f32[1,1,256]{2,1,0:T(1,128)} %copy-done.47) | copy-start | bytes 3076
  167.6 14.3 %copy-start.50 = (f32[1,1,256]{2,1,0:T(1,128)S(1)}, f32[1,1,256]{2,1,0:T(1,128)}, u32[]{:S(2)}) copy-start(f32[1,1,256]{2,1,0:T(1,128)} %copy-done.49) | copy-start | bytes 3076
  (42 other events, 85.2 us)
Sparse Core Ops, SparseCore 0:
  166.3 99.0 all-reduce.3
where the time goes:
time: 276 us
  waiting for transfers between devices  103 us (37%)
  blocking collectives  62.4 us (23%)
  other arithmetic  46.5 us (17%)
  matrix products  20.2 us (7%)
  local copies, waits for them, and re-layouts  19.3 us (7%)
  between operations  15.5 us (6%)
  starting transfers between devices  8.82 us (3%)
    psum x1, waiting for transfers between devices, per_device(): lax.psum((kernel_part, w_in_part, w_out_part, hidden_bias_part, channel_p...  72.9 us
    psum x1, blocking collectives, per_device(): lax.psum((kernel_part, w_in_part, w_out_part, hidden_bias_part, channel_p...  62.4 us
    ppermute x2, waiting for transfers between devices, with_halo(): lax.ppermute(tail, axis, [(i, (i + 1) % count) for i in range(ends)])  30 us
    reduce_sum x6, other arithmetic, kernel_terms(): cells_list.append(jnp.sum(window * grad_map, axis=(0, 1, 2)))  13.4 us
    reduce_sum x1, other arithmetic, per_device(): center = jnp.mean(conv_out, axis=-1, keepdims=True)  9.86 us
    convert_element_type x1, other arithmetic, per_device(): (upstream + apply_taps(grad_padded, kernel[::-1, ::-1], height, breadth))...  9.55 us
    unnamed x211, local copies, waits for them, and re-layouts  7.31 us
    ppermute x2, starting transfers between devices, with_halo(): lax.ppermute(tail, axis, [(i, (i + 1) % count) for i in range(ends)])  6.2 us
  transfers between devices with their start and end apart: 5, of which 3 were waited for; matrix products, arithmetic and copies ran while one was open for 5% of the time, Pallas kernels for 0%

commit v1 on v0

--- a/solution.py
+++ b/solution.py
@@ -135,7 +135,8 @@
     )
     channel_part = jnp.stack([conv_bias_part, gain_part, nbias_part, out_bias_part, scale_part])
     kernel_sum, w_in_sum, w_out_sum, hidden_sum, channel_sum = lax.psum(
-        (kernel_part, w_in_part, w_out_part, hidden_bias_part, channel_part), ("tile", "draw")
+        lax.psum((kernel_part, w_in_part, w_out_part, hidden_bias_part, channel_part), "draw"),
+        "tile",
     )
     total_cells = inputs.shape[0] * lax.axis_size("draw") * height * lax.axis_size("tile") * breadth
     factor = 1.0 / jnp.sqrt(jnp.float32(total_cells))

time: 276 us -> 263 us (0.953)
  blocking collectives: 62.4 us -> 46.1 us
  starting transfers between devices: 8.82 us -> 12 us
    psum x0 -> x1, waiting for transfers between devices: none -> 87.7 us  [per_device(): lax.psum(lax.psum((kernel_part, w_in_part, w_out_part, hidden_bias_part,...]
    psum x1, waiting for transfers between devices: 72.9 us -> 0.01 us  [per_device(): lax.psum((kernel_part, w_in_part, w_out_part, hidden_bias_part, channel_p...]
    psum x1, blocking collectives: 62.4 us -> 3.56 us  [per_device(): lax.psum((kernel_part, w_in_part, w_out_part, hidden_bias_part, channel_p...]
    psum x0 -> x1, blocking collectives: none -> 42.6 us  [per_device(): lax.psum(lax.psum((kernel_part, w_in_part, w_out_part, hidden_bias_part,...]
    ppermute x2, waiting for transfers between devices: 30 us -> 16.2 us  [with_halo(): lax.ppermute(tail, axis, [(i, (i + 1) % count) for i in range(ends)])]
    ppermute x2, starting transfers between devices: 6.2 us -> 9.31 us  [with_halo(): lax.ppermute(tail, axis, [(i, (i + 1) % count) for i in range(ends)])]
    unnamed x211 -> x221, local copies, waits for them, and re-layouts: 7.31 us -> 8.51 us
  transfers between devices with their start and end apart: 5 -> 6, of which waited for: 3 -> 2; matrix products, arithmetic and copies ran while one was open for 5% -> 5% of each run, Pallas kernels for 0% -> 0%
where the time goes in v1:
time: 263 us
  waiting for transfers between devices  104 us (40%)
  other arithmetic  47.1 us (18%)
  blocking collectives  46.1 us (18%)
  matrix products  20.2 us (8%)
  local copies, waits for them, and re-layouts  17.9 us (7%)
  between operations  15.6 us (6%)
  starting transfers between devices  12 us (5%)
    psum x1, waiting for transfers between devices, per_device(): lax.psum(lax.psum((kernel_part, w_in_part, w_out_part, hidden_bias_part,...  87.7 us
    psum x1, blocking collectives, per_device(): lax.psum(lax.psum((kernel_part, w_in_part, w_out_part, hidden_bias_part,...  42.6 us
    ppermute x2, waiting for transfers between devices, with_halo(): lax.ppermute(tail, axis, [(i, (i + 1) % count) for i in range(ends)])  16.2 us
    reduce_sum x6, other arithmetic, kernel_terms(): cells_list.append(jnp.sum(window * grad_map, axis=(0, 1, 2)))  13.9 us
    reduce_sum x1, other arithmetic, per_device(): center = jnp.mean(conv_out, axis=-1, keepdims=True)  9.86 us
    convert_element_type x1, other arithmetic, per_device(): (upstream + apply_taps(grad_padded, kernel[::-1, ::-1], height, breadth))...  9.55 us
    ppermute x2, starting transfers between devices, with_halo(): lax.ppermute(tail, axis, [(i, (i + 1) % count) for i in range(ends)])  9.31 us
    unnamed x221, local copies, waits for them, and re-layouts  8.51 us
  transfers between devices with their start and end apart: 6, of which 2 were waited for; matrix products, arithmetic and copies ran while one was open for 5% of the time, Pallas kernels for 0%

profile of v1, /device:TPU:0, one launch (start us, length us, event | category | flops | bytes accessed | tf_op | source)
XLA Modules:
  0.0 262.8 jit_solution(14347774652418739383)
XLA Ops:
  7.2 0.0 copy-start
  7.2 0.0 all-reduce.9.cloned.1.call-start
  7.2 1.2 copy.24
  8.4 0.0 copy-start.9
  8.4 0.0 copy-start.51
  8.4 0.1 fusion.237
  8.5 4.9 %collective-permute-start = (bf16[1,3,270,256]{3,2,1,0:T(8,128)(2,1)S(1)}, bf16[1,3,270,256]{3,2,1,0:T(8,128)(2,1)S(1)}, u32[]{:S(2)}, u32[]{:S(2)}) collective-permute-start(bf16[1,3,270,256]{3,2,1,0:T(8,128)(2,1)S(1)} %get-tuple-element.96), channel_id=1, source_target_pairs={{0,2},{2,4},{4,6},{6,8},{8,10},{10,12},{12,14},{1,3},{3,5},{5,7},{... | collective-permute-start | bytes 1244168 | tf_op jit(solution)/shard_map/ppermute | solution.py:19
  13.4 1.3 collective-permute-start.1
  15.0 16.2 %collective-permute-done = bf16[1,3,270,256]{3,2,1,0:T(8,128)(2,1)S(1)} collective-permute-done((bf16[1,3,270,256]{3,2,1,0:T(8,128)(2,1)S(1)}, bf16[1,3,270,256]{3,2,1,0:T(8,128)(2,1)S(1)}, u32[]{:S(2)}, u32[]{:S(2)}) %collective-permute-start) | collective-permute-done | bytes 414752 | tf_op jit(solution)/shard_map/ppermute | solution.py:19
  31.2 0.2 maximum_convert_fusion
  31.7 9.9 %fusion.233 = (f32[4,270]{1,0:T(4,128)S(1)}, f32[1,4,270,256]{3,2,1,0:T(8,128)S(1)}) fusion(f32[256]{0:T(256)S(1)} %copy-done.95, f32[256]{0:T(256)S(1)} %bitcast.185, f32[1,10,3,256]{3,2,1,0:T(4,128)S(1)} %get-tuple-element.89, f32[1,10,270,256]{3,2,1,0:T(8,128)S(1)} %maximum_convert_fusion, f32[256]{0:T(256)S(1)} %bitcast.187, f32[256]{0:T(256)S(1)} %bitcast.131, ...), kind=kLoop, calls=%fused_computation.447 | loop fusion | flops 38982600 | bytes 11827424 | tf_op jit(solution)/shard_map/reduce_sum | solution.py:87
  41.6 0.0 copy-start.96
  41.6 0.5 multiply_reduce_fusion.2
  42.1 0.5 copy-done.3
  42.5 1.2 add_convert_fusion
  43.7 2.0 reshape.497
  45.7 4.8 %multiply_convert_fusion = (bf16[1080,1024]{1,0:T(8,128)(2,1)S(1)}, f32[1080,1024]{1,0:T(8,128)}) fusion(f32[1024]{0:T(1024)S(1)} %copy-done.101, bf16[1080,256]{1,0:T(8,128)(2,1)} %reshape.497, bf16[256,1024]{1,0:T(8,128)(2,1)S(1)} %copy-done), kind=kOutput, calls=%fused_computation.140 | convolution fusion | flops 577290240 | bytes 7716864 | tf_op jit(solution)/shard_map/dot_general | solution.py:92
  50.6 1.4 copy-done.104
  52.0 1.9 convolution_add_fusion.1
  53.8 2.5 reshape.498
  56.3 3.6 %fusion.11 = (f32[256]{0:T(256)}, bf16[1,4,270,256]{3,2,1,0:T(8,128)(2,1)}, f32[256]{0:T(256)}, bf16[1,4,270,256]{3,2,1,0:T(8,128)(2,1)}) fusion(f32[1,4,270,256]{3,2,1,0:T(8,128)} %reshape.498, f32[4,270]{1,0:T(4,128)S(1)} %convert_element_type.63, bf16[1,4,270,256]{3,1,2,0:T(4,128)(2,1)} %param.23, f32[256]{0:T(256)S(1)} %copy-done.97, ...), kind=kLoop, calls=%fused_computation.154 | loop fusion | flops 3593728 | bytes 3325152 | tf_op jit(solution)/shard_map/reduce_sum | solution.py:101
  60.0 2.0 reshape.499
  62.0 3.7 %fusion.242 = f32[1024,256]{1,0:T(8,128)} fusion(bf16[1080,1024]{1,0:T(8,128)(2,1)} %copy-done.104, bf16[1080,256]{1,0:T(8,128)(2,1)} %reshape.499), kind=kOutput, calls=%fused_computation.456 | convolution fusion | flops 566231040 | bytes 3813376 | tf_op jit(solution)/shard_map/dot_general | solution.py:104
  65.8 3.8 %convert_reduce_fusion.1 = (f32[1024]{0:T(1024)}, bf16[1080,1024]{1,0:T(8,128)(2,1)S(1)}) fusion(f32[1080,1024]{1,0:T(8,128)S(1)} %copy-done.105, bf16[1080,256]{1,0:T(8,128)(2,1)S(1)} %copy-done.8, bf16[1024,256]{1,0:T(8,128)(2,1)S(1)} %copy-done.100), kind=kOutput, calls=%fused_computation.139 | convolution fusion | flops 589454336 | bytes 7716864 | tf_op jit(solution)/shard_map/dot_general | solution.py:107
  69.6 1.4 copy-done.103
  71.0 1.9 fusion.241
  72.9 4.0 %fusion.231 = (f32[256]{0:T(256)}, f32[1080]{0:T(1024)S(1)}, f32[1080,256]{1,0:T(8,128)}) fusion(f32[256]{0:T(256)S(1)} %copy-done.10, bf16[1080,1024]{1,0:T(8,128)(2,1)} %copy-done.103, bf16[256,1024]{1,0:T(8,128)(2,1)S(1)} %copy-done), kind=kOutput, calls=%fused_computation.446 | convolution fusion | flops 567059136 | bytes 3848416 | tf_op jit(solution)/shard_map/dot_general | solution.py:115
  76.9 2.4 reshape.500
  79.2 2.8 %multiply_reduce_fusion = (f32[256]{0:T(256)}, f32[4,270]{1,0:T(4,128)S(1)}) fusion(f32[1,4,270,256]{3,2,1,0:T(8,128)} %reshape.500, f32[1,4,270,256]{3,2,1,0:T(8,128)} %copy-done.3, f32[4,270]{1,0:T(4,128)S(1)} %add_rsqrt_fusion, f32[4,270]{1,0:T(4,128)S(1)} %broadcast_multiply_fusion.6, f32[256]{0:T(256)S(1)} %copy-done.10), kind=kLoop, calls=%fused_computation.422 | loop fusion | flops 1934024 | bytes 2226848 | tf_op jit(solution)/shard_map/reduce_sum | solution.py:118
  82.0 0.1 div.17
  82.1 2.6 fusion.57
  84.7 2.1 fusion.55
  86.7 2.4 fusion.59
  89.1 2.3 fusion.60
  91.4 2.0 fusion.56
  93.5 2.5 fusion.58
  96.0 0.0 copy-start.93
  96.1 0.1 fusion.236
  96.1 0.5 copy-done.77
  96.7 0.0 copy-done.80
  96.7 0.0 copy-done.93
  96.8 4.4 %collective-permute-start.2 = (bf16[1,3,270,256]{3,2,1,0:T(8,128)(2,1)S(1)}, bf16[1,3,270,256]{3,2,1,0:T(8,128)(2,1)S(1)}, u32[]{:S(2)}, u32[]{:S(2)}) collective-permute-start(bf16[1,3,270,256]{3,2,1,0:T(8,128)(2,1)S(1)} %get-tuple-element.94), channel_id=1, source_target_pairs={{0,2},{2,4},{4,6},{6,8},{8,10},{10,12},{12,14},{1,3},{3,5},{5,7},{... | collective-permute-start | bytes 1244168 | tf_op jit(solution)/shard_map/ppermute | solution.py:19
  101.2 1.3 collective-permute-start.3
  102.5 1.1 copy.29
  103.9 0.0 all-reduce.9.cloned.1.call-update
  103.9 0.0 all-reduce.7.cloned.1.call-start
  104.0 0.3 copy-done.52
  104.2 0.0 copy-done.53
  104.3 0.0 copy-done.54
  104.3 0.0 copy-done.98
  104.9 3.6 %all-reduce.2 = (f32[7,7,256]{2,1,0:T(8,128)S(1)}, f32[1024]{0:T(1024)S(1)}, f32[5,256]{1,0:T(8,128)S(1)}) all-reduce(f32[7,7,256]{2,1,0:T(8,128)S(1)} %constant_dynamic-update-slice_fusion, f32[1024]{0:T(1024)S(1)} %copy-done.82, f32[5,256]{1,0:T(8,128)S(1)} %stack.279), channel_id=1, replica_groups=mesh['group'=2,'tile'=8,'draw'=2] {'draw'}, use_global_device_ids=true, to_apply=%region_53.0 | all-reduce | flops 14848 | bytes 118784 | tf_op jit(solution)/shard_map/psum | solution.py:138
  108.4 42.6 %all-reduce = (f32[7,7,256]{2,1,0:T(8,128)S(1)}, f32[1024]{0:T(1024)S(1)}, f32[5,256]{1,0:T(8,128)S(1)}) all-reduce(f32[7,7,256]{2,1,0:T(8,128)S(1)} %get-tuple-element.75, f32[1024]{0:T(1024)S(1)} %get-tuple-element.76, f32[5,256]{1,0:T(8,128)S(1)} %get-tuple-element.77), channel_id=1, replica_groups=mesh['group'=2,'tile'=8,'draw'=2] {'tile'}, use_global_device_ids=true, to_apply=%region_54.0 | all-reduce | flops 14848 | bytes 118784 | tf_op jit(solution)/shard_map/psum | solution.py:137
  151.0 0.6 broadcast_multiply_fusion.3
  151.6 0.6 broadcast_multiply_fusion.7
  152.2 0.6 broadcast_multiply_fusion.2
  152.8 0.0 all-reduce.7.cloned.1.call-update
  152.9 0.0 copy-start.5
  153.1 0.2 maximum_convert_fusion.1
  153.3 0.6 copy-done.5
  154.1 9.5 %fusion.9 = bf16[1,4,270,256]{3,2,1,0:T(8,128)(2,1)S(1)} fusion(f32[1,10,3,256]{3,2,1,0:T(4,128)S(1)} %get-tuple-element.87, f32[1,10,270,256]{3,2,1,0:T(8,128)S(1)} %maximum_convert_fusion.1, f32[1,10,3,256]{3,2,1,0:T(4,128)S(1)} %get-tuple-element.86, f32[256]{0:T(256)S(1)} %bitcast.186, f32[256]{0:T(256)S(1)} %bitcast.188, f32[256]{0:T(256)S(1)} %bitcast.132, ...), kind=kLoop, calls=%fused_computation.152 | loop fusion | flops 39260160 | bytes 11822080 | tf_op jit(solution)/shard_map/convert_element_type | solution.py:133
  163.6 1.1 copy.30
  164.7 87.7 %all-reduce.7.cloned.1.call-done = (f32[256,1024]{1,0:T(8,128)}, f32[1024,256]{1,0:T(8,128)}) async-done(((f32[256,1024]{1,0:T(8,128)}, f32[1024,256]{1,0:T(8,128)}), (f32[256,1024]{1,0:T(8,128)}, f32[1024,256]{1,0:T(8,128)})) %all-reduce.7.cloned.1.call-update) | async-done | bytes 2097168 | tf_op jit(solution)/shard_map/psum | solution.py:137
  252.5 2.4 broadcast_multiply_fusion
  254.8 1.1 broadcast_multiply_fusion.1
  (224 shorter events, 0.8 us)
Async XLA Ops:
  7.2 38.5 %copy-start = (bf16[256,1024]{1,0:T(8,128)(2,1)S(1)}, bf16[256,1024]{1,0:T(8,128)(2,1)}, u32[]{:S(2)}) copy-start(bf16[256,1024]{1,0:T(8,128)(2,1)} %param.18) | copy-start | bytes 1572868
  7.2 145.7 %all-reduce.9.cloned.1.call-start = ((), (), s32[]{:S(2)}) async-start(), calls=%async_computation.1 | async-start | bytes 4194304 | tf_op jit(solution)/shard_map/psum | solution.py:138
  8.4 6.3 %copy-start.9 = (f32[7,7,256]{2,1,0:T(8,128)S(1)}, f32[7,7,256]{2,1,0:T(8,128)}, u32[]{:S(2)}) copy-start(f32[7,7,256]{2,1,0:T(8,128)} %param.14) | copy-start | bytes 150532
  8.4 6.3 %copy-start.51 = (s32[4,270]{1,0:T(4,128)S(1)}, s32[4,270]{1,0:T(4,128)}, u32[]{:S(2)}) copy-start(s32[4,270]{1,0:T(4,128)} %param.13) | copy-start | bytes 12964
  8.5 22.7 %collective-permute-start = (bf16[1,3,270,256]{3,2,1,0:T(8,128)(2,1)S(1)}, bf16[1,3,270,256]{3,2,1,0:T(8,128)(2,1)S(1)}, u32[]{:S(2)}, u32[]{:S(2)}) collective-permute-start(bf16[1,3,270,256]{3,2,1,0:T(8,128)(2,1)S(1)} %get-tuple-element.96), channel_id=1, source_target_pairs={{0,2},{2,4},{4,6},{6,8},{8,10},{10,12},{12,14},{1,3},{3,5},{5,7},{... | collective-permute-start | bytes 1244168 | tf_op jit(solution)/shard_map/ppermute | solution.py:19
  13.4 17.8 %collective-permute-start.1 = (bf16[1,3,270,256]{3,2,1,0:T(8,128)(2,1)S(1)}, bf16[1,3,270,256]{3,2,1,0:T(8,128)(2,1)S(1)}, u32[]{:S(2)}, u32[]{:S(2)}) collective-permute-start(bf16[1,3,270,256]{3,2,1,0:T(8,128)(2,1)S(1)} %get-tuple-element.97), channel_id=1, source_target_pairs={{2,0},{4,2},{6,4},{8,6},{10,8},{12,10},{14,12},{3,1},{5,3},{7,5},{... | collective-permute-start | bytes 1244168 | tf_op jit(solution)/shard_map/ppermute | solution.py:21
  14.8 16.7 %copy-start.11 = (f32[1,1,256]{2,1,0:T(1,128)}, f32[1,1,256]{2,1,0:T(1,128)S(1)}, u32[]{:S(2)}) copy-start(f32[1,1,256]{2,1,0:T(1,128)S(1)} %get-tuple-element.146) | copy-start | bytes 3076
  14.8 16.7 %copy-start.13 = (f32[1,1,256]{2,1,0:T(1,128)}, f32[1,1,256]{2,1,0:T(1,128)S(1)}, u32[]{:S(2)}) copy-start(f32[1,1,256]{2,1,0:T(1,128)S(1)} %get-tuple-element.117) | copy-start | bytes 3076
  14.8 16.7 %copy-start.15 = (f32[1,1,256]{2,1,0:T(1,128)}, f32[1,1,256]{2,1,0:T(1,128)S(1)}, u32[]{:S(2)}) copy-start(f32[1,1,256]{2,1,0:T(1,128)S(1)} %get-tuple-element.118) | copy-start | bytes 3076
  14.8 16.7 %copy-start.17 = (f32[1,1,256]{2,1,0:T(1,128)}, f32[1,1,256]{2,1,0:T(1,128)S(1)}, u32[]{:S(2)}) copy-start(f32[1,1,256]{2,1,0:T(1,128)S(1)} %get-tuple-element.119) | copy-start | bytes 3076
  14.8 16.7 %copy-start.19 = (f32[1,1,256]{2,1,0:T(1,128)}, f32[1,1,256]{2,1,0:T(1,128)S(1)}, u32[]{:S(2)}) copy-start(f32[1,1,256]{2,1,0:T(1,128)S(1)} %get-tuple-element.120) | copy-start | bytes 3076
  14.9 16.7 %copy-start.21 = (f32[1,1,256]{2,1,0:T(1,128)}, f32[1,1,256]{2,1,0:T(1,128)S(1)}, u32[]{:S(2)}) copy-start(f32[1,1,256]{2,1,0:T(1,128)S(1)} %get-tuple-element.121) | copy-start | bytes 3076
  14.9 16.7 %copy-start.23 = (f32[1,1,256]{2,1,0:T(1,128)}, f32[1,1,256]{2,1,0:T(1,128)S(1)}, u32[]{:S(2)}) copy-start(f32[1,1,256]{2,1,0:T(1,128)S(1)} %get-tuple-element.122) | copy-start | bytes 3076
  14.9 16.7 %copy-start.25 = (f32[1,1,256]{2,1,0:T(1,128)}, f32[1,1,256]{2,1,0:T(1,128)S(1)}, u32[]{:S(2)}) copy-start(f32[1,1,256]{2,1,0:T(1,128)S(1)} %get-tuple-element.123) | copy-start | bytes 3076
  14.9 16.7 %copy-start.27 = (f32[1,1,256]{2,1,0:T(1,128)}, f32[1,1,256]{2,1,0:T(1,128)S(1)}, u32[]{:S(2)}) copy-start(f32[1,1,256]{2,1,0:T(1,128)S(1)} %get-tuple-element.124) | copy-start | bytes 3076
  14.9 16.7 %copy-start.29 = (f32[1,1,256]{2,1,0:T(1,128)}, f32[1,1,256]{2,1,0:T(1,128)S(1)}, u32[]{:S(2)}) copy-start(f32[1,1,256]{2,1,0:T(1,128)S(1)} %get-tuple-element.125) | copy-start | bytes 3076
  14.9 16.7 %copy-start.31 = (f32[1,1,256]{2,1,0:T(1,128)}, f32[1,1,256]{2,1,0:T(1,128)S(1)}, u32[]{:S(2)}) copy-start(f32[1,1,256]{2,1,0:T(1,128)S(1)} %get-tuple-element.126) | copy-start | bytes 3076
  14.9 16.7 %copy-start.33 = (f32[1,1,256]{2,1,0:T(1,128)}, f32[1,1,256]{2,1,0:T(1,128)S(1)}, u32[]{:S(2)}) copy-start(f32[1,1,256]{2,1,0:T(1,128)S(1)} %get-tuple-element.127) | copy-start | bytes 3076
  14.9 16.7 %copy-start.35 = (f32[1,1,256]{2,1,0:T(1,128)}, f32[1,1,256]{2,1,0:T(1,128)S(1)}, u32[]{:S(2)}) copy-start(f32[1,1,256]{2,1,0:T(1,128)S(1)} %get-tuple-element.128) | copy-start | bytes 3076
  14.9 16.7 %copy-start.37 = (f32[1,1,256]{2,1,0:T(1,128)}, f32[1,1,256]{2,1,0:T(1,128)S(1)}, u32[]{:S(2)}) copy-start(f32[1,1,256]{2,1,0:T(1,128)S(1)} %get-tuple-element.129) | copy-start | bytes 3076
  14.9 16.7 %copy-start.39 = (f32[1,1,256]{2,1,0:T(1,128)}, f32[1,1,256]{2,1,0:T(1,128)S(1)}, u32[]{:S(2)}) copy-start(f32[1,1,256]{2,1,0:T(1,128)S(1)} %get-tuple-element.130) | copy-start | bytes 3076
  15.0 16.7 %copy-start.41 = (f32[1,1,256]{2,1,0:T(1,128)}, f32[1,1,256]{2,1,0:T(1,128)S(1)}, u32[]{:S(2)}) copy-start(f32[1,1,256]{2,1,0:T(1,128)S(1)} %get-tuple-element.131) | copy-start | bytes 3076
  15.0 16.7 %copy-start.43 = (f32[1,1,256]{2,1,0:T(1,128)}, f32[1,1,256]{2,1,0:T(1,128)S(1)}, u32[]{:S(2)}) copy-start(f32[1,1,256]{2,1,0:T(1,128)S(1)} %get-tuple-element.132) | copy-start | bytes 3076
  15.0 16.7 %copy-start.45 = (f32[1,1,256]{2,1,0:T(1,128)}, f32[1,1,256]{2,1,0:T(1,128)S(1)}, u32[]{:S(2)}) copy-start(f32[1,1,256]{2,1,0:T(1,128)S(1)} %get-tuple-element.133) | copy-start | bytes 3076
  15.0 16.7 %copy-start.47 = (f32[1,1,256]{2,1,0:T(1,128)}, f32[1,1,256]{2,1,0:T(1,128)S(1)}, u32[]{:S(2)}) copy-start(f32[1,1,256]{2,1,0:T(1,128)S(1)} %get-tuple-element.134) | copy-start | bytes 3076
  15.0 16.7 %copy-start.49 = (f32[1,1,256]{2,1,0:T(1,128)}, f32[1,1,256]{2,1,0:T(1,128)S(1)}, u32[]{:S(2)}) copy-start(f32[1,1,256]{2,1,0:T(1,128)S(1)} %get-tuple-element.135) | copy-start | bytes 3076
  15.0 16.7 %copy-start.95 = (f32[256]{0:T(256)S(1)}, f32[256]{0:T(256)}, u32[]{:S(2)}) copy-start(f32[256]{0:T(256)} %param.15) | copy-start | bytes 3076
  42.5 3.2 %copy-start.101 = (f32[1024]{0:T(1024)S(1)}, f32[1024]{0:T(1024)}, u32[]{:S(2)}) copy-start(f32[1024]{0:T(1024)} %param.19) | copy-start | bytes 12292
  45.7 6.2 %copy-start.99 = (bf16[1024,256]{1,0:T(8,128)(2,1)S(1)}, bf16[1024,256]{1,0:T(8,128)(2,1)}, u32[]{:S(2)}) copy-start(bf16[1024,256]{1,0:T(8,128)(2,1)} %param.20) | copy-start | bytes 1572868
  45.7 6.2 %copy-start.102 = (f32[256]{0:T(256)S(1)}, f32[256]{0:T(256)}, u32[]{:S(2)}) copy-start(f32[256]{0:T(256)} %param.21) | copy-start | bytes 3076
  50.6 1.4 copy-start.104
  53.8 2.5 copy-start.97
  62.0 3.8 %copy-start.8 = (bf16[1080,256]{1,0:T(8,128)(2,1)S(1)}, bf16[1080,256]{1,0:T(8,128)(2,1)}, u32[]{:S(2)}) copy-start(bf16[1080,256]{1,0:T(8,128)(2,1)} %reshape.499) | copy-start | bytes 1658884
  62.0 3.8 %copy-start.100 = (bf16[1024,256]{1,0:T(8,128)(2,1)S(1)}, bf16[1024,256]{1,0:T(8,128)(2,1)}, u32[]{:S(2)}) copy-start(bf16[1024,256]{1,0:T(8,128)(2,1)} %param.20) | copy-start | bytes 1572868
  62.0 3.8 %copy-start.105 = (f32[1080,1024]{1,0:T(8,128)S(1)}, f32[1080,1024]{1,0:T(8,128)}, u32[]{:S(2)}) copy-start(f32[1080,1024]{1,0:T(8,128)} %get-tuple-element.148) | copy-start | bytes 13271044
  65.7 5.2 %copy-start.7 = (bf16[1080,256]{1,0:T(8,128)(2,1)S(1)}, bf16[1080,256]{1,0:T(8,128)(2,1)}, u32[]{:S(2)}) copy-start(bf16[1080,256]{1,0:T(8,128)(2,1)} %reshape.497) | copy-start | bytes 1658884
  69.6 1.4 copy-start.103
  84.7 11.3 %copy-start.1 = (bf16[1,4,270,256]{3,2,1,0:T(8,128)(2,1)}, bf16[1,4,270,256]{3,2,1,0:T(8,128)(2,1)S(1)}, u32[]{:S(2)}) copy-start(bf16[1,4,270,256]{3,2,1,0:T(8,128)(2,1)S(1)} %get-tuple-element.83) | copy-start | bytes 1658884
  96.1 6.4 %copy-start.4 = (bf16[1,4,270,256]{3,2,1,0:T(8,128)(2,1)S(1)}, bf16[1,4,270,256]{3,2,1,0:T(8,128)(2,1)}, u32[]{:S(2)}) copy-start(bf16[1,4,270,256]{3,2,1,0:T(8,128)(2,1)} %get-tuple-element.91) | copy-start | bytes 1658884
  96.8 56.3 %collective-permute-start.2 = (bf16[1,3,270,256]{3,2,1,0:T(8,128)(2,1)S(1)}, bf16[1,3,270,256]{3,2,1,0:T(8,128)(2,1)S(1)}, u32[]{:S(2)}, u32[]{:S(2)}) collective-permute-start(bf16[1,3,270,256]{3,2,1,0:T(8,128)(2,1)S(1)} %get-tuple-element.94), channel_id=1, source_target_pairs={{0,2},{2,4},{4,6},{6,8},{8,10},{10,12},{12,14},{1,3},{3,5},{5,7},{... | collective-permute-start | bytes 1244168 | tf_op jit(solution)/shard_map/ppermute | solution.py:19
  101.2 51.9 %collective-permute-start.3 = (bf16[1,3,270,256]{3,2,1,0:T(8,128)(2,1)S(1)}, bf16[1,3,270,256]{3,2,1,0:T(8,128)(2,1)S(1)}, u32[]{:S(2)}, u32[]{:S(2)}) collective-permute-start(bf16[1,3,270,256]{3,2,1,0:T(8,128)(2,1)S(1)} %get-tuple-element.95), channel_id=1, source_target_pairs={{2,0},{4,2},{6,4},{8,6},{10,8},{12,10},{14,12},{3,1},{5,3},{7,5},{... | collective-permute-start | bytes 1244168 | tf_op jit(solution)/shard_map/ppermute | solution.py:21
  103.9 148.5 %all-reduce.7.cloned.1.call-start = ((), (), s32[]{:S(2)}) async-start(), calls=%async_computation | async-start | bytes 4194304 | tf_op jit(solution)/shard_map/psum | solution.py:137
  151.6 1.5 copy-start.2
  152.9 1.1 copy-start.5
  152.9 1.0 copy-start.12
  152.9 1.0 copy-start.14
  152.9 1.0 copy-start.16
  152.9 1.0 copy-start.18
  152.9 1.0 copy-start.20
  152.9 1.0 copy-start.22
  152.9 1.0 copy-start.24
  152.9 1.0 copy-start.26
  152.9 1.0 copy-start.28
  153.0 1.0 copy-start.30
  153.0 1.0 copy-start.32
  153.0 1.0 copy-start.34
  153.0 1.0 copy-start.36
  153.0 1.0 copy-start.38
  153.0 1.0 copy-start.40
  153.0 1.0 copy-start.42
  153.0 1.0 copy-start.44
  153.0 1.0 copy-start.46
  153.0 1.0 copy-start.48
  252.5 2.4 copy-start.6
  (48 other events, 37.7 us)
Sparse Core Ops, SparseCore 0:
  104.1 24.4 all-reduce.8
  153.0 99.4 all-reduce.6
